TPU v7x, 1024 devices: a whole 4x4x32 slice. The times are simulated.
1024 devices in a mesh: replica: 64 (over z, core), tensor: 16 (over x, y).
Axes of the slice: x: 4, y: 4, z: 32, core: 2. Of those that a mesh axis runs over, the one named last changes fastest.
Arguments:
- activations: bfloat16 [16384, 4096], P('replica'), may hold values from -6 to 6
- out_grads: bfloat16 [16384, 4096], P('replica', 'tensor'), may hold values from -1 to 1
- query_weight: bfloat16 [4096, 4096], P(None, 'tensor'), may hold values from -0.375 to 0.375
- carried_q: float32 [4096, 64], P('tensor'), may hold values from -6 to 6
Outputs:
- input_grads: bfloat16 [16384, 4096], P(('replica', 'tensor'))
- q_summed: float32 [4096, 64], P('tensor')
- new_error: bfloat16 [64, 4096, 4096], P('replica', None, 'tensor')
All inputs are finite; a program needn't handle non-finite values.
Results may differ from a plain program's by a relative error of at most 0.014.
Values may be sent and summed in bfloat16 or wider, within the bound.
A program may use at most 64 MiB of HBM per device.

v0:
```python
import jax
import jax.numpy as jnp
from jax import lax
from jax.sharding import PartitionSpec as P


def triangular_apply(gram_matrix, p_part):
    cholesky_factor = jnp.linalg.cholesky(gram_matrix)
    return jax.scipy.linalg.solve_triangular(cholesky_factor, p_part.T, lower=True).T


def shards(activations, out_grads, query_weight, carried_q):
    highest = lax.Precision.HIGHEST
    replicas = lax.axis_size("replica")
    gradient = lax.dot_general(
        activations, out_grads, (((0,), (0,)), ((), ())), preferred_element_type=jnp.float32
    )
    p_local = jnp.dot(gradient, carried_q, precision=highest, preferred_element_type=jnp.float32)
    p_whole = lax.psum(p_local, "replica")
    gram_matrix = jnp.dot(p_whole.T, p_whole, precision=highest, preferred_element_type=jnp.float32)
    p_orth = triangular_apply(gram_matrix, p_whole)
    q_local = lax.dot_general(
        gradient,
        p_orth,
        (((0,), (0,)), ((), ())),
        precision=highest,
        preferred_element_type=jnp.float32,
    )
    q_summed = lax.psum(q_local, "replica")
    decompressed = jnp.dot(
        p_orth, q_summed.T, precision=highest, preferred_element_type=jnp.float32
    )
    new_error = (gradient - decompressed / replicas).astype(jnp.bfloat16)[None]
    summed = lax.psum_scatter(
        lax.dot_general(
            out_grads, query_weight, (((1,), (1,)), ((), ())), preferred_element_type=jnp.float32
        ).astype(jnp.bfloat16),
        "tensor",
        scatter_dimension=0,
        tiled=True,
    )
    return (summed, q_summed, new_error)


def solution(mesh):
    in_specs = (P("replica", None), P("replica", "tensor"), P(None, "tensor"), P("tensor", None))
    out_specs = (P(("replica", "tensor"), None), P("tensor", None), P("replica", None, "tensor"))
    return jax.shard_map(shards, mesh=mesh, in_specs=in_specs, out_specs=out_specs, check_vma=False)
```

profile of v0, /device:TPU:25, one launch (start us, length us, event | category | flops | bytes accessed | tf_op | source)
XLA Modules:
  0.0 824.4 jit_solution(1589922972979030319)
XLA Ops:
  8.0 0.0 copy-start
  8.0 0.0 copy-start.4
  8.0 0.0 all-reduce.3.cloned.1.call-start
  8.1 1.5 copy-done
  9.6 1.7 fusion.7
  11.3 0.0 copy-start.1
  11.3 1.9 copy-done.1
  13.2 0.0 copy-done.4
  13.2 5.2 fusion.8
  18.3 0.0 all-reduce.3.cloned.1.call-update
  18.4 0.0 all-reduce.5.cloned.1.call-start
  18.4 414.1 %all-reduce.3.cloned.1.call-done = f32[4096,64]{0,1:T(8,128)} async-done(((f32[4096,64]{0,1:T(8,128)}), f32[4096,64]{0,1:T(8,128)}) %all-reduce.3.cloned.1.call-update) | async-done | bytes 1048592 | tf_op jit(solution)/shard_map/psum | solution.py:19
  432.5 2.5 fusion.9
  435.0 0.0 copy-start.2
  435.1 0.1 copy.7
  435.2 5.8 cholesky.16
  441.0 0.6 compare_reduce_fusion
  441.7 0.7 fusion.3
  442.3 4.9 custom-call.7
  447.2 2.3 fusion.4
  449.5 5.4 fusion.10
  454.9 0.0 all-reduce.5.cloned.1.call-update
  454.9 0.2 reduce-scatter.2.cloned.1.call-start
  455.1 0.0 copy-done.2
  455.1 3.7 convolution_convert_fusion
  458.8 0.0 reduce-scatter.2.cloned.1.call-update
  458.8 350.8 %all-reduce.5.cloned.1.call-done = f32[256,64]{0,1:T(8,128)} async-done(((f32[256,64]{0,1:T(8,128)}), f32[256,64]{0,1:T(8,128)}) %all-reduce.5.cloned.1.call-update) | async-done | bytes 65552 | tf_op jit(solution)/shard_map/psum | solution.py:29
  809.6 0.0 copy-start.3
  809.6 6.7 fusion.2
  816.3 0.0 reduce-scatter.2.cloned.1.call-done
  816.3 0.0 copy-done.3
  816.3 0.6 copy.10
  (2 shorter events, 0.0 us)
Async XLA Ops:
  8.0 1.6 copy-start
  8.0 5.2 copy-start.4
  8.0 424.5 %all-reduce.3.cloned.1.call-start = ((), (), s32[]{:S(2)}) async-start(), calls=%async_computation.2 | async-start | bytes 2097152 | tf_op jit(solution)/shard_map/psum | solution.py:19
  11.3 1.9 copy-start.1
  18.4 791.3 %all-reduce.5.cloned.1.call-start = ((), (), s32[]{:S(2)}) async-start(), calls=%async_computation.3 | async-start | bytes 131072 | tf_op jit(solution)/shard_map/psum | solution.py:29
  435.0 20.1 %copy-start.2 = (bf16[256,256]{1,0:T(8,128)(2,1)S(1)}, bf16[256,256]{1,0:T(8,128)(2,1)}, u32[]{:S(2)}) copy-start(bf16[256,256]{1,0:T(8,128)(2,1)} %param.5) | copy-start | bytes 393220
  454.9 361.4 %reduce-scatter.2.cloned.1.call-start = ((), (), s32[]{:S(2)}) async-start(), calls=%async_computation.1 | async-start | bytes 2228224 | tf_op jit(solution)/shard_map/reduce_scatter | solution.py:34
  809.6 6.7 copy-start.3
Sparse Core Ops, SparseCore 0:
  18.5 413.9 all-reduce.2
  455.0 354.5 all-reduce.4
Sparse Core Ops, SparseCore 1:
  461.2 107.1 reduce-scatter.1
where the time goes:
time: 826 us; the launch traced here: 824 us
  waiting for transfers between devices  765 us (93%)
  matrix products  27.3 us (3%)
  between operations  15.6 us (2%)
  other arithmetic  12.1 us (1%)
    psum x1, waiting for transfers between devices, shards(): p_whole = lax.psum(p_local, 'replica')  414 us
    psum x1, waiting for transfers between devices, shards(): q_summed = lax.psum(q_local, 'replica')  351 us
  transfers between devices with their start and end apart: 3, of which 2 were waited for; matrix products, arithmetic and copies ran while one was open for 1% of the time, Pallas kernels for 0%

commit v1 on v0

v1 whole, which is shorter than its diff:
```python
import functools

import jax
import jax.numpy as jnp
from jax import lax
from jax.experimental import pallas as pl
from jax.experimental.pallas import tpu as pltpu
from jax.sharding import PartitionSpec as P

MESH = pl.DeviceIdType.MESH
F32 = jnp.float32
BF16 = jnp.bfloat16

D_WIN = 4096
COLS = 256
TOK = 256
RANK = 64
CHIPS = 32
WIN = 8
GROUPS = CHIPS // WIN
PEERS = 16
BLK = D_WIN // (2 * WIN)
ROWS = TOK // PEERS

NEAR = (-4, 3, -3, 2, -2, 1, -1)
FAR = (16, 8, 24)


def dot(a, b, dims, precision=None):
    return lax.dot_general(a, b, (dims, ((), ())), precision=precision, preferred_element_type=F32)


def halves(x):
    high = x.astype(BF16)
    return high, (x - high.astype(F32)).astype(BF16)


def kernel(
    act_hbm, grad_hbm, weight_hbm, q_hbm,
    summed_hbm, q_out_hbm, error_hbm,
    act, og, weight, carried, gradient, part, from_peers, summed,
    p_send, p_acc, p_pair, near_send, near_recv, mid, p_full, p_cols, aug,
    s_send, s_pair, s_acc, s_near_recv, s_mid, s_full, q_out, error,
    load_sems, act_sems, store_sems, peer_send, peer_recv,
    pair_sems, near_s, near_r, mid_s, mid_r, gather_s, gather_r, pass_s, pass_r,
    s_pair_sems, s_near_s, s_near_r, s_mid_s, s_mid_r, s_gather_s, s_gather_r, s_pass_s, s_pass_r,
):
    replica = lax.axis_index("replica")
    tensor = lax.axis_index("tensor")
    chip = replica // 2
    core = lax.rem(replica, 2)
    other = 1 - core
    mine = lax.rem(chip, WIN)
    group = chip // WIN

    def at(offset):
        return (lax.rem(chip + offset + CHIPS, CHIPS) * 2 + core, tensor)

    partner = (chip * 2 + other, tensor)

    def peer(offset):
        return (replica, lax.rem(tensor + offset, PEERS))

    def remote(src, dst, send, recv, device):
        return pltpu.make_async_remote_copy(
            src_ref=src, dst_ref=dst, send_sem=send, recv_sem=recv, device_id=device, device_id_type=MESH
        )

    barrier = pltpu.get_barrier_semaphore()
    friends = [at(o) for o in FAR + (-4, 4, -3, 3, -2, 2, -1, 1)]
    friends += [peer(o) for o in range(1, PEERS)] + [partner]
    for friend in friends:
        pl.semaphore_signal(barrier, inc=1, device_id=friend, device_id_type=MESH)

    load_og = pltpu.make_async_copy(grad_hbm, og, load_sems.at[0])
    load_q = pltpu.make_async_copy(q_hbm, carried, load_sems.at[1])
    load_weight = pltpu.make_async_copy(weight_hbm, weight, load_sems.at[2])
    load_og.start()
    load_q.start()

    def load_act(index):
        half, j = index // WIN, lax.rem(index, WIN)
        b = 2 * j + lax.rem(half + other, 2)
        return pltpu.make_async_copy(act_hbm.at[:, pl.ds(b * BLK, BLK)], act.at[b], act_sems.at[index])

    @pl.loop(0, 2 * WIN)
    def _(i):
        load_act(i).start()

    load_weight.start()

    load_og.wait()
    load_q.wait()
    q_high, q_low = halves(carried[...])
    y2 = dot(jnp.concatenate([q_high, q_low], axis=0), og[...], ((1,), (1,)))
    y_high, y_low = halves(y2[:RANK] + y2[RANK:])
    y_parts = jnp.concatenate([y_high, y_low], axis=0)

    def p_block(i, b):
        load_act(i).wait()
        both = dot(y_parts, act[b], ((1,), (0,)))
        return both[:RANK] + both[RANK:]

    @pl.loop(0, WIN)
    def _(j):
        p_send[j] = p_block(j, 2 * j + other).astype(BF16)

    @pl.loop(0, WIN)
    def _(j):
        p_acc[j] = p_block(WIN + j, 2 * j + core)

    pl.semaphore_wait(barrier, len(friends))

    pair = remote(p_send, p_pair, pair_sems.at[0], pair_sems.at[1], partner)
    pair.start()

    load_weight.wait()

    @pl.loop(0, D_WIN // COLS)
    def _(b):
        rows = pl.ds(pl.multiple_of(b * COLS, COLS), COLS)
        part[:, rows] = dot(og[...], weight[rows, :], ((1,), (1,))).astype(BF16)

    pair.wait_recv()
    sends = []
    for k, e in enumerate(NEAR):
        j = lax.rem(chip + e + CHIPS, WIN)
        near_send[k] = (p_acc[j] + p_pair[j].astype(F32)).astype(BF16)
        copy = remote(near_send.at[k], near_recv.at[k], near_s.at[k], near_r.at[k], at(e))
        copy.start()
        sends.append(copy)

    peer_copies = []
    for o in range(1, PEERS):
        to = lax.rem(tensor + o, PEERS)
        copy = remote(
            part.at[pl.ds(pl.multiple_of(to * ROWS, ROWS), ROWS)], from_peers.at[tensor],
            peer_send.at[o - 1], peer_recv.at[o - 1], peer(o),
        )
        copy.start()
        peer_copies.append(copy)

    total = p_acc[mine] + p_pair[mine].astype(F32)
    for k in reversed(range(len(NEAR))):
        sends[k].wait_recv()
        total += near_recv[k].astype(F32)

    mid[group] = total.astype(BF16)
    mid_copies = []
    for k, o in enumerate(FAR):
        copy = remote(mid.at[group], mid.at[group], mid_s.at[k], mid_r.at[k], at(o))
        copy.start()
        mid_copies.append(copy)

    @pl.loop(0, D_WIN // BLK)
    def _(b):
        gradient[b] = dot(act[b], og[...], ((0,), (0,)))

    for copy in mid_copies:
        copy.wait_recv()
    chunk = mid[0].astype(F32)
    for g in range(1, GROUPS):
        chunk += mid[g].astype(F32)
    p_full[core, mine] = chunk.astype(BF16)

    def gather_from(k):
        return lax.rem(chip + NEAR[k] + CHIPS, WIN)

    gathers, passes = [], []
    for k, e in enumerate(NEAR):
        copy = remote(
            p_full.at[core, mine], p_full.at[core, mine], gather_s.at[k], gather_r.at[k], at(-e)
        )
        copy.start()
        gathers.append(copy)

    def hand_on(k, j):
        copy = remote(p_full.at[core, j], p_full.at[core, j], pass_s.at[k], pass_r.at[k], partner)
        copy.start()
        passes.append(copy)

    hand_on(len(NEAR), mine)

    def z_gram(half, j, carry):
        z, gram = carry
        block = p_full[half, j]
        return (
            z + dot(block, act[2 * j + half], ((1,), (1,))),
            gram + dot(block, block, ((1,), (1,))),
        )

    carry = (jnp.zeros((RANK, TOK), F32), jnp.zeros((RANK, RANK), F32))
    order = list(reversed(range(len(NEAR))))
    for k in order:
        remote(
            p_full.at[core, gather_from(k)], p_full.at[core, gather_from(k)],
            gather_s.at[k], gather_r.at[k], at(NEAR[k]),
        ).wait_recv()
        hand_on(k, gather_from(k))
    for k in [len(NEAR)] + order:
        j = mine if k == len(NEAR) else gather_from(k)
        remote(
            p_full.at[other, j], p_full.at[other, j], pass_s.at[k], pass_r.at[k], partner
        ).wait_recv()

    def z_step(i, carry):
        return z_gram(i // WIN, lax.rem(i, WIN), carry)

    z, gram = lax.fori_loop(0, 2 * WIN, z_step, carry)

    z_high, z_low = halves(z)
    s2 = dot(jnp.concatenate([z_high, z_low], axis=0), og[...], ((1,), (0,)))
    s = s2[:RANK] + s2[RANK:]
    half_cols = COLS // 2
    s_send[0] = s[:, :half_cols]
    s_send[1] = s[:, half_cols:]
    s_pair_copy = remote(s_send.at[other], s_pair, s_pair_sems.at[0], s_pair_sems.at[1], partner)
    s_pair_copy.start()
    lane = lax.broadcasted_iota(jnp.int32, (RANK, 2 * RANK), 1)
    row = lax.broadcasted_iota(jnp.int32, (RANK, 2 * RANK), 0)
    aug[:, :] = jnp.concatenate([gram, (lane == row)[:, :RANK].astype(F32)], axis=1)
    s_pair_copy.wait_recv()
    s_acc[...] = s_send[core] + s_pair[...]

    s_sends = []
    for k, e in enumerate(NEAR):
        j = lax.rem(chip + e + CHIPS, WIN)
        copy = remote(
            s_acc.at[pl.ds(pl.multiple_of(j * 8, 8), 8)], s_near_recv.at[k], s_near_s.at[k], s_near_r.at[k], at(e)
        )
        copy.start()
        s_sends.append(copy)

    s_total = s_acc[pl.ds(pl.multiple_of(mine * 8, 8), 8)]
    for k in order:
        s_sends[k].wait_recv()
        s_total += s_near_recv[k]
    s_mid[group] = s_total
    s_mid_copies = []
    for k, o in enumerate(FAR):
        copy = remote(s_mid.at[group], s_mid.at[group], s_mid_s.at[k], s_mid_r.at[k], at(o))
        copy.start()
        s_mid_copies.append(copy)

    def eliminate(k, c):
        m = aug[...]
        pivot_row = aug[pl.ds(k, 1), :]
        column = jnp.sum(jnp.where(lane == k, m, 0.0), axis=1, keepdims=True)
        pivot = jnp.sum(jnp.where(lane[:1] == k, pivot_row, 0.0), axis=1, keepdims=True)
        factor = jnp.where(row[:, :1] > k, column, 0.0)
        aug[...] = m - factor * (pivot_row / pivot)
        return c

    lax.fori_loop(0, RANK, eliminate, 0)
    m = aug[...]
    diagonal = jnp.sum(jnp.where(lane == row, m, 0.0), axis=1, keepdims=True)
    l_inverse = (m / jnp.sqrt(diagonal))[:, RANK:]

    @pl.loop(0, 2 * WIN)
    def _(b):
        block = p_full[lax.rem(b, 2), b // 2].astype(F32)
        p_cols[b] = jnp.concatenate([block, block], axis=0).T.astype(BF16)

    for copy in s_mid_copies:
        copy.wait_recv()
    s_chunk = s_mid[0]
    for g in range(1, GROUPS):
        s_chunk += s_mid[g]
    s_full[core, mine] = s_chunk
    s_gathers, s_passes = [], []
    for k, e in enumerate(NEAR):
        copy = remote(
            s_full.at[core, mine], s_full.at[core, mine], s_gather_s.at[k], s_gather_r.at[k], at(-e)
        )
        copy.start()
        s_gathers.append(copy)

    def s_hand_on(k, j):
        copy = remote(s_full.at[core, j], s_full.at[core, j], s_pass_s.at[k], s_pass_r.at[k], partner)
        copy.start()
        s_passes.append(copy)

    s_hand_on(len(NEAR), mine)

    from_peers[tensor] = part[pl.ds(pl.multiple_of(tensor * ROWS, ROWS), ROWS), :]
    for copy in peer_copies:
        copy.wait_recv()

    @pl.loop(0, D_WIN // 512)
    def _(i):
        columns = pl.ds(pl.multiple_of(i * 512, 512), 512)
        acc = from_peers[0, :, columns].astype(F32)
        for t in range(1, PEERS):
            acc += from_peers[t, :, columns].astype(F32)
        summed[:, columns] = acc.astype(BF16)

    store_summed = pltpu.make_async_copy(summed, summed_hbm, store_sems.at[0])
    store_summed.start()

    for k in order:
        j = gather_from(k)
        remote(
            s_full.at[core, j], s_full.at[core, j], s_gather_s.at[k], s_gather_r.at[k], at(NEAR[k])
        ).wait_recv()
        s_hand_on(k, j)
    for k in [len(NEAR)] + order:
        j = mine if k == len(NEAR) else gather_from(k)
        remote(
            s_full.at[other, j], s_full.at[other, j], s_pass_s.at[k], s_pass_r.at[k], partner
        ).wait_recv()

    highest = lax.Precision.HIGHEST
    s_whole = jnp.concatenate([s_full[0].reshape(RANK, half_cols), s_full[1].reshape(RANK, half_cols)], axis=1)
    q_t = dot(l_inverse, s_whole, ((1,), (0,)), highest)
    q_out[...] = q_t
    store_q = pltpu.make_async_copy(q_out, q_out_hbm, store_sems.at[1])
    store_q.start()
    right = dot(l_inverse, q_t, ((0,), (0,)), highest) * (1.0 / (2 * CHIPS))
    right_high, right_low = halves(right)
    right_parts = jnp.concatenate([right_high, right_low], axis=0)

    def store_error(b):
        rows = pl.ds(b * BLK, BLK)
        return pltpu.make_async_copy(error.at[rows], error_hbm.at[rows], store_sems.at[2 + b])

    @pl.loop(0, 2 * WIN)
    def _(b):
        rows = pl.ds(pl.multiple_of(b * BLK, BLK), BLK)
        error[rows, :] = (gradient[b] - dot(p_cols[b], right_parts, ((1,), (0,)))).astype(BF16)
        store_error(b).start()

    for copy in [pair] + sends + mid_copies + gathers + passes + peer_copies:
        copy.wait_send()
    for copy in [s_pair_copy] + s_sends + s_mid_copies + s_gathers + s_passes:
        copy.wait_send()
    store_summed.wait()
    store_q.wait()

    @pl.loop(0, 2 * WIN)
    def _(b):
        store_error(b).wait()


def shards(activations, out_grads, query_weight, carried_q):
    any_space = pl.BlockSpec(memory_space=pl.ANY)
    dma = pltpu.SemaphoreType.DMA
    near = len(NEAR)
    far = len(FAR)
    summed, q_summed, error = pl.pallas_call(
        kernel,
        out_shape=(
            jax.ShapeDtypeStruct((ROWS, D_WIN), BF16),
            jax.ShapeDtypeStruct((RANK, COLS), F32),
            jax.ShapeDtypeStruct((D_WIN, COLS), BF16),
        ),
        in_specs=[any_space] * 4,
        out_specs=(any_space,) * 3,
        scratch_shapes=[
            pltpu.VMEM((2 * WIN, TOK, BLK), BF16),
            pltpu.VMEM((TOK, COLS), BF16),
            pltpu.VMEM((D_WIN, COLS), BF16),
            pltpu.VMEM((RANK, COLS), F32),
            pltpu.VMEM((2 * WIN, BLK, COLS), F32),
            pltpu.VMEM((TOK, D_WIN), BF16),
            pltpu.VMEM((PEERS, ROWS, D_WIN), BF16),
            pltpu.VMEM((ROWS, D_WIN), BF16),
            pltpu.VMEM((WIN, RANK, BLK), BF16),
            pltpu.VMEM((WIN, RANK, BLK), F32),
            pltpu.VMEM((WIN, RANK, BLK), BF16),
            pltpu.VMEM((near, RANK, BLK), BF16),
            pltpu.VMEM((near, RANK, BLK), BF16),
            pltpu.VMEM((GROUPS, RANK, BLK), BF16),
            pltpu.VMEM((2, WIN, RANK, BLK), BF16),
            pltpu.VMEM((2 * WIN, BLK, 2 * RANK), BF16),
            pltpu.VMEM((RANK, 2 * RANK), F32),
            pltpu.VMEM((2, RANK, COLS // 2), F32),
            pltpu.VMEM((RANK, COLS // 2), F32),
            pltpu.VMEM((RANK, COLS // 2), F32),
            pltpu.VMEM((near, RANK // WIN, COLS // 2), F32),
            pltpu.VMEM((GROUPS, RANK // WIN, COLS // 2), F32),
            pltpu.VMEM((2, WIN, RANK // WIN, COLS // 2), F32),
            pltpu.VMEM((RANK, COLS), F32),
            pltpu.VMEM((D_WIN, COLS), BF16),
            dma((3,)), dma((2 * WIN,)), dma((2 + 2 * WIN,)),
            dma((PEERS - 1,)), dma((PEERS - 1,)),
            dma((2,)),
            dma((near,)), dma((near,)),
            dma((far,)), dma((far,)),
            dma((near,)), dma((near,)),
            dma((near + 1,)), dma((near + 1,)),
            dma((2,)),
            dma((near,)), dma((near,)),
            dma((far,)), dma((far,)),
            dma((near,)), dma((near,)),
            dma((near + 1,)), dma((near + 1,)),
        ],
        compiler_params=pltpu.CompilerParams(
            collective_id=0, has_side_effects=True, vmem_limit_bytes=48 * 1024 * 1024
        ),
        name="powersgd",
    )(activations, out_grads, query_weight, carried_q.T)
    return summed, q_summed.T, error[None]


def solution(mesh):
    in_specs = (P("replica", None), P("replica", "tensor"), P(None, "tensor"), P("tensor", None))
    out_specs = (P(("replica", "tensor"), None), P("tensor", None), P("replica", None, "tensor"))
    return jax.shard_map(shards, mesh=mesh, in_specs=in_specs, out_specs=out_specs, check_vma=False)
```

time: 826 us -> 107 us (0.13)
  waiting for transfers between devices: 765 us -> 0 us
  Pallas kernels: 0 us -> 99.3 us
  matrix products: 27.3 us -> 0 us
  between operations: 15.6 us -> 0.65 us
  other arithmetic: 12.1 us -> 0 us
    psum x2 -> x0, waiting for transfers between devices: 765 us -> none  [the longest x1 414 us: shards(): p_whole = lax.psum(p_local, 'replica')]
    pallas_call x0 -> x1, Pallas kernels: none -> 99.3 us  [shards(): pl.pallas_call(kernel, out_shape=(jax.ShapeDtypeStruct((ROWS, D_WIN), BF1...]
    dot_general x6 -> x0, matrix products: 25 us -> none  [the longest x1 6.67 us: shards(): jnp.dot(p_orth, q_summed.T, precision=highest, preferred_element_type=jnp...]
    another operation x5 -> x0, other arithmetic: 12.1 us -> none  [the longest x3 6.52 us: triangular_apply(): cholesky_factor = jnp.linalg.cholesky(gram_matrix)]
  transfers between devices with their start and end apart: 3 -> 0, of which waited for: 2 -> 0; matrix products, arithmetic and copies ran while one was open for 1% -> 0% of each run, Pallas kernels for 0% -> 0%
where the time goes in v1:
time: 107 us; the launch traced here: 106 us
  Pallas kernels  99.3 us (93%)
  local copies, waits for them, and re-layouts  5.93 us (6%)
    pallas_call x1, Pallas kernels, shards(): pl.pallas_call(kernel, out_shape=(jax.ShapeDtypeStruct((ROWS, D_WIN), BF1...  99.3 us
    unnamed x9, local copies, waits for them, and re-layouts  5.93 us

profile of v1, /device:TPU:25, one launch (start us, length us, event | category | flops | bytes accessed | tf_op | source)
XLA Modules:
  0.0 105.9 jit_solution(4384312744556816261)
XLA Ops:
  0.6 0.0 copy-start
  0.6 1.6 %copy-done = bf16[256,4096]{1,0:T(8,128)(2,1)S(1)} copy-done((bf16[256,4096]{1,0:T(8,128)(2,1)S(1)}, bf16[256,4096]{1,0:T(8,128)(2,1)}, u32[]{:S(2)}) %copy-start) | copy-done | bytes 2097176
  2.2 0.0 copy-start.1
  2.2 0.9 copy-done.1
  3.1 0.0 copy-start.2
  3.1 0.8 copy-done.2
  4.0 99.3 %powersgd.1 = (bf16[16,4096]{1,0:T(8,128)(2,1)S(1)}, f32[64,256]{1,0:T(8,128)S(1)}, bf16[4096,256]{1,0:T(8,128)(2,1)S(1)}) custom-call(bf16[256,4096]{1,0:T(8,128)(2,1)S(1)} %copy-done, bf16[256,256]{1,0:T(8,128)(2,1)S(1)} %copy-done.1, bf16[4096,256]{1,0:T(8,128)(2,1)} %weight_hbm.1, f32[64,256]{1,0:T(8,128)S(1)} %bitcast.4), custom_call_target="tpu_custom_call" | custom-call | tf_op jit(solution)/shard_map/powersgd/pallas_call | solution.py:349
  103.3 0.7 copy.10
  104.0 0.6 copy.11
  104.6 1.3 %copy.12 = bf16[1,4096,256]{2,1,0:T(8,128)(2,1)} copy(bf16[1,4096,256]{2,1,0:T(8,128)(2,1)S(1)} %bitcast.3) | data formatting | bytes 4194304
Async XLA Ops:
  0.6 1.6 %copy-start = (bf16[256,4096]{1,0:T(8,128)(2,1)S(1)}, bf16[256,4096]{1,0:T(8,128)(2,1)}, u32[]{:S(2)}) copy-start(bf16[256,4096]{1,0:T(8,128)(2,1)} %act_hbm.1) | copy-start | bytes 6291460
  2.2 0.9 copy-start.1
  3.1 0.8 copy-start.2

commit v2 on v1

v2 whole, which is shorter than its diff:
```python
import jax
import jax.numpy as jnp
from jax import lax
from jax.experimental import pallas as pl
from jax.experimental.pallas import tpu as pltpu
from jax.sharding import PartitionSpec as P

MESH = pl.DeviceIdType.MESH
F32 = jnp.float32
BF16 = jnp.bfloat16

D_WIN = 4096
COLS = 256
TOK = 256
RANK = 64
CHIPS = 32
WIN = 8
GROUPS = CHIPS // WIN
PEERS = 16
BLK = D_WIN // (2 * WIN)
ROWS = TOK // PEERS

HALF = RANK // 2
S_WIN = 4
S_ROWS = RANK // (2 * S_WIN)

NEAR = (-4, 3, -3, 2, -2, 1, -1)
FAR = (16, 8, 24)
S_NEAR = (-2, 1, -1)
S_FAR = (16, 12, 20, 8, 24, 4, 28)


def dot(a, b, dims, precision=None):
    return lax.dot_general(a, b, (dims, ((), ())), precision=precision, preferred_element_type=F32)


def halves(x):
    high = x.astype(BF16)
    return high, (x - high.astype(F32)).astype(BF16)


def kernel(
    act_hbm, grad_hbm, weight_hbm, q_hbm,
    summed_hbm, q_out_hbm, error_hbm,
    act, og, weight, carried, gradient, part, from_peers, summed,
    p_send, p_acc, p_pair, near_send, near_recv, mid, p_full, p_cols, z, gram, aug, apply_ref,
    s_all, s_near_recv, s_mid, s_full, right_parts, q_out, error,
    load_sems, act_sems, store_sems, peer_send, peer_recv,
    pair_s, pair_r, near_s, near_r, mid_s, mid_r, gather_s, gather_r, pass_s, pass_r,
    s_near_s, s_near_r, s_mid_s, s_mid_r, s_gather_s, s_gather_r,
):
    replica = lax.axis_index("replica")
    tensor = lax.axis_index("tensor")
    chip = replica // 2
    core = lax.rem(replica, 2)
    other = 1 - core
    sign = 1 - 2 * core
    mine = lax.rem(chip, WIN)
    group = chip // WIN

    def chip_at(offset):
        return lax.rem(chip + offset + CHIPS, CHIPS)

    def at(offset, on=None):
        return (chip_at(offset) * 2 + (core if on is None else on), tensor)

    partner = at(0, other)

    def peer(offset):
        return (replica, lax.rem(tensor + offset, PEERS))

    def remote(src, dst, send, recv, device):
        return pltpu.make_async_remote_copy(
            src_ref=src, dst_ref=dst, send_sem=send, recv_sem=recv, device_id=device, device_id_type=MESH
        )

    load_og = pltpu.make_async_copy(grad_hbm, og, load_sems.at[0])
    load_q = pltpu.make_async_copy(q_hbm, carried, load_sems.at[1])
    load_weight = pltpu.make_async_copy(weight_hbm, weight, load_sems.at[2])
    load_og.start()
    load_q.start()

    def load_act(index):
        half, j = index // WIN, lax.rem(index, WIN)
        b = 2 * j + lax.rem(half + other, 2)
        return pltpu.make_async_copy(act_hbm.at[:, pl.ds(b * BLK, BLK)], act.at[b], act_sems.at[index])

    @pl.loop(0, 2 * WIN)
    def _(i):
        load_act(i).start()

    barrier = pltpu.get_barrier_semaphore()
    friends = [at(o) for o in (16, 12, -12, 8, -8, 4, -4, 3, -3, 2, -2, 1, -1)]
    friends += [at(o, other) for o in (2, -2, 1, -1)] + [partner]
    friends += [peer(o) for o in range(1, PEERS)]
    for friend in friends:
        pl.semaphore_signal(barrier, inc=1, device_id=friend, device_id_type=MESH)

    load_weight.start()

    load_og.wait()
    load_q.wait()
    q_high, q_low = halves(carried[...])
    y2 = dot(jnp.concatenate([q_high, q_low], axis=0), og[...], ((1,), (1,)))
    y_high, y_low = halves(y2[:RANK] + y2[RANK:])
    y_parts = jnp.concatenate([y_high, y_low], axis=0)

    def p_blocks(first, start, half, out):
        for j in range(first, first + WIN // 2):
            load_act(start + j).wait()
        for j in range(first, first + WIN // 2):
            both = dot(y_parts, act[2 * j + half], ((1,), (0,)))
            block = (both[:RANK] + both[RANK:]).astype(out.dtype)
            out[0, j] = block[:HALF]
            out[1, j] = block[HALF:]

    for start, half, out in ((0, other, p_send), (WIN, core, p_acc)):
        for first in (0, WIN // 2):
            p_blocks(first, start, half, out)

    pl.semaphore_wait(barrier, len(friends))

    pairs = []
    for h in range(2):
        copy = remote(p_send.at[h], p_pair.at[h], pair_s.at[h], pair_r.at[h], partner)
        copy.start()
        pairs.append(copy)

    sends = []
    for h in range(2):
        pairs[h].wait_recv()
        for k, e in enumerate(NEAR):
            j = lax.rem(chip_at(sign * e), WIN)
            near_send[h, k] = (p_acc[h, j] + p_pair[h, j].astype(F32)).astype(BF16)
            copy = remote(near_send.at[h, k], near_recv.at[h, k], near_s.at[h, k], near_r.at[h, k], at(sign * e))
            copy.start()
            sends.append(copy)

    load_weight.wait()

    @pl.loop(0, D_WIN // COLS, unroll=4)
    def _(b):
        rows = pl.ds(pl.multiple_of(b * COLS, COLS), COLS)
        part[:, rows] = dot(og[...], weight[rows, :], ((1,), (1,))).astype(BF16)

    peer_copies = []
    for o in range(1, PEERS):
        to = lax.rem(tensor + o, PEERS)
        copy = remote(
            part.at[pl.ds(pl.multiple_of(to * ROWS, ROWS), ROWS)], from_peers.at[tensor],
            peer_send.at[o - 1], peer_recv.at[o - 1], peer(o),
        )
        copy.start()
        peer_copies.append(copy)

    order = list(reversed(range(len(NEAR))))
    mid_copies = []
    for h in range(2):
        total = p_acc[h, mine] + p_pair[h, mine].astype(F32)
        for k in order:
            sends[h * len(NEAR) + k].wait_recv()
            total += near_recv[h, k].astype(F32)
        mid[h, group] = total.astype(BF16)
        for k, o in enumerate(FAR):
            copy = remote(mid.at[h, group], mid.at[h, group], mid_s.at[h, k], mid_r.at[h, k], at(o))
            copy.start()
            mid_copies.append(copy)

    @pl.loop(0, D_WIN // BLK, unroll=4)
    def _(b):
        gradient[b] = dot(act[b], og[...], ((0,), (0,)))

    def gather_from(k):
        return lax.rem(chip_at(sign * NEAR[k]), WIN)

    gathers, passes = [], []

    def hand_on(h, k, j):
        copy = remote(p_full.at[core, j, h], p_full.at[core, j, h], pass_s.at[h, k], pass_r.at[h, k], partner)
        copy.start()
        passes.append(copy)

    for h in range(2):
        for k in range(len(FAR)):
            mid_copies[h * len(FAR) + k].wait_recv()
        chunk = mid[h, 0].astype(F32)
        for g in range(1, GROUPS):
            chunk += mid[h, g].astype(F32)
        p_full[core, mine, h] = chunk.astype(BF16)
        for k, e in enumerate(NEAR):
            copy = remote(
                p_full.at[core, mine, h], p_full.at[core, mine, h], gather_s.at[h, k], gather_r.at[h, k],
                at(-sign * e),
            )
            copy.start()
            gathers.append(copy)
        hand_on(h, len(NEAR), mine)

    def p_whole(half, j):
        return p_full[half, j].reshape(RANK, BLK)

    def z_gram(half, j):
        block = p_whole(half, j)
        z[...] += dot(block, act[2 * j + half], ((1,), (1,)))
        gram[...] += dot(block, block, ((1,), (1,)))

    z[...] = jnp.zeros_like(z)
    gram[...] = jnp.zeros_like(gram)
    for h in range(2):
        for k in order:
            j = gather_from(k)
            remote(
                p_full.at[core, j, h], p_full.at[core, j, h], gather_s.at[h, k], gather_r.at[h, k],
                at(sign * NEAR[k]),
            ).wait_recv()
            hand_on(h, k, j)
    for k in [len(NEAR)] + order:
        j = mine if k == len(NEAR) else gather_from(k)
        z_gram(core, j)
    for k in [len(NEAR)] + order:
        j = mine if k == len(NEAR) else lax.rem(chip_at(-sign * NEAR[k]), WIN)
        for h in range(2):
            remote(
                p_full.at[other, j, h], p_full.at[other, j, h], pass_s.at[h, k], pass_r.at[h, k], partner
            ).wait_recv()
        z_gram(other, j)

    z_high, z_low = halves(z[...])
    s2 = dot(jnp.concatenate([z_high, z_low], axis=0), og[...], ((1,), (0,)))
    s_all[...] = s2[:RANK] + s2[RANK:]

    s_targets = [(e, core) for e in S_NEAR] + [(e, other) for e in S_NEAR] + [(0, other)]

    def s_chunk_of(chip_index, on):
        return 2 * lax.rem(chip_index, S_WIN) + on

    def s_rows(i):
        return pl.ds(pl.multiple_of(i * S_ROWS, S_ROWS), S_ROWS)

    s_mine = s_chunk_of(chip, core)
    s_group = chip // S_WIN
    s_sends = []
    for k, (e, on) in enumerate(s_targets):
        copy = remote(
            s_all.at[s_rows(s_chunk_of(chip_at(sign * e), on))], s_near_recv.at[k],
            s_near_s.at[k], s_near_r.at[k], at(sign * e, on),
        )
        copy.start()
        s_sends.append(copy)

    lane = lax.broadcasted_iota(jnp.int32, (RANK, 2 * RANK), 1)
    row = lax.broadcasted_iota(jnp.int32, (RANK, 2 * RANK), 0)
    aug[...] = jnp.concatenate([gram[...], (lane == row)[:, :RANK].astype(F32)], axis=1)

    @pl.loop(0, 2 * WIN, unroll=4)
    def _(b):
        block = p_whole(lax.rem(b, 2), b // 2)
        p_cols[b] = jnp.concatenate([block, block], axis=0).T

    s_total = s_all[s_rows(s_mine)]
    for k in reversed(range(len(s_targets))):
        s_sends[k].wait_recv()
        s_total += s_near_recv[k]
    s_mid[s_group] = s_total
    s_mid_copies = []
    for k, o in enumerate(S_FAR):
        copy = remote(s_mid.at[s_group], s_mid.at[s_group], s_mid_s.at[k], s_mid_r.at[k], at(o))
        copy.start()
        s_mid_copies.append(copy)

    def eliminate(k, c):
        m = aug[...]
        pivot_row = aug[pl.ds(k, 1), :]
        column = jnp.sum(jnp.where(lane == k, m, 0.0), axis=1, keepdims=True)
        pivot = jnp.sum(jnp.where(lane[:1] == k, pivot_row, 0.0), axis=1, keepdims=True)
        factor = jnp.where(row[:, :1] > k, column, 0.0)
        aug[...] = m - factor * (pivot_row / pivot)
        return c

    lax.fori_loop(0, RANK, eliminate, 0)
    m = aug[...]
    diagonal = jnp.sum(jnp.where(lane == row, m, 0.0), axis=1, keepdims=True)
    l_inverse = (m / jnp.sqrt(diagonal))[:, RANK:]
    highest = lax.Precision.HIGHEST
    apply = jnp.concatenate(
        [l_inverse, dot(l_inverse, l_inverse, ((0,), (0,)), highest) * (1.0 / (2 * CHIPS))], axis=0
    )

    apply_ref[...] = apply
    for copy in s_mid_copies:
        copy.wait_recv()
    s_chunk = s_mid[0]
    for g in range(1, CHIPS // S_WIN):
        s_chunk += s_mid[g]
    s_full[s_mine] = s_chunk
    s_gathers = []
    for k, (e, on) in enumerate(s_targets):
        copy = remote(
            s_full.at[s_mine], s_full.at[s_mine], s_gather_s.at[k], s_gather_r.at[k], at(-sign * e, on)
        )
        copy.start()
        s_gathers.append(copy)
    from_peers[tensor] = part[pl.ds(pl.multiple_of(tensor * ROWS, ROWS), ROWS), :]
    for copy in peer_copies:
        copy.wait_recv()

    @pl.loop(0, D_WIN // 512, unroll=2)
    def _(i):
        columns = pl.ds(pl.multiple_of(i * 512, 512), 512)
        acc = from_peers[0, :, columns].astype(F32)
        for t in range(1, PEERS):
            acc += from_peers[t, :, columns].astype(F32)
        summed[:, columns] = acc.astype(BF16)

    store_summed = pltpu.make_async_copy(summed, summed_hbm, store_sems.at[0])
    store_summed.start()

    for k in reversed(range(len(s_targets))):
        e, on = s_targets[k]
        toward = sign * e if k < len(S_NEAR) else -sign * e
        i = s_chunk_of(chip_at(toward), on)
        remote(
            s_full.at[i], s_full.at[i], s_gather_s.at[k], s_gather_r.at[k], at(toward, on)
        ).wait_recv()

    both = dot(apply_ref[...], s_full[...].reshape(RANK, COLS), ((1,), (0,)), highest)
    right_high, right_low = halves(both[RANK:])
    right_parts[...] = jnp.concatenate([right_high, right_low], axis=0)

    q_out[...] = both[:RANK]
    store_q = pltpu.make_async_copy(q_out, q_out_hbm, store_sems.at[1])
    store_q.start()

    def store_error(g):
        rows = pl.ds(g * 4 * BLK, 4 * BLK)
        return pltpu.make_async_copy(error.at[rows], error_hbm.at[rows], store_sems.at[2 + g])

    for g in range(WIN // 2):
        for b in range(4 * g, 4 * g + 4):
            product = dot(p_cols[b], right_parts[...], ((1,), (0,)))
            error[pl.ds(b * BLK, BLK), :] = (gradient[b] - product).astype(BF16)
        store_error(g).start()

    for copy in pairs + sends + mid_copies + gathers + passes + peer_copies + s_sends + s_mid_copies + s_gathers:
        copy.wait_send()
    store_summed.wait()
    store_q.wait()

    for g in range(WIN // 2):
        store_error(g).wait()


def shards(activations, out_grads, query_weight, carried_q):
    in_hbm = pl.BlockSpec(memory_space=pltpu.HBM)
    dma = pltpu.SemaphoreType.DMA
    near, far, s_near, s_far = len(NEAR), len(FAR), 2 * len(S_NEAR) + 1, len(S_FAR)
    summed, q_summed, error = pl.pallas_call(
        kernel,
        out_shape=(
            jax.ShapeDtypeStruct((ROWS, D_WIN), BF16),
            jax.ShapeDtypeStruct((RANK, COLS), F32),
            jax.ShapeDtypeStruct((D_WIN, COLS), BF16),
        ),
        in_specs=[in_hbm] * 4,
        out_specs=(pl.BlockSpec(memory_space=pl.ANY),) * 3,
        scratch_shapes=[
            pltpu.VMEM((2 * WIN, TOK, BLK), BF16),
            pltpu.VMEM((TOK, COLS), BF16),
            pltpu.VMEM((D_WIN, COLS), BF16),
            pltpu.VMEM((RANK, COLS), F32),
            pltpu.VMEM((2 * WIN, BLK, COLS), F32),
            pltpu.VMEM((TOK, D_WIN), BF16),
            pltpu.VMEM((PEERS, ROWS, D_WIN), BF16),
            pltpu.VMEM((ROWS, D_WIN), BF16),
            pltpu.VMEM((2, WIN, HALF, BLK), BF16),
            pltpu.VMEM((2, WIN, HALF, BLK), F32),
            pltpu.VMEM((2, WIN, HALF, BLK), BF16),
            pltpu.VMEM((2, near, HALF, BLK), BF16),
            pltpu.VMEM((2, near, HALF, BLK), BF16),
            pltpu.VMEM((2, GROUPS, HALF, BLK), BF16),
            pltpu.VMEM((2, WIN, 2, HALF, BLK), BF16),
            pltpu.VMEM((2 * WIN, BLK, 2 * RANK), BF16),
            pltpu.VMEM((RANK, TOK), F32),
            pltpu.VMEM((RANK, RANK), F32),
            pltpu.VMEM((RANK, 2 * RANK), F32),
            pltpu.VMEM((2 * RANK, RANK), F32),
            pltpu.VMEM((RANK, COLS), F32),
            pltpu.VMEM((s_near, S_ROWS, COLS), F32),
            pltpu.VMEM((CHIPS // S_WIN, S_ROWS, COLS), F32),
            pltpu.VMEM((2 * S_WIN, S_ROWS, COLS), F32),
            pltpu.VMEM((2 * RANK, COLS), BF16),
            pltpu.VMEM((RANK, COLS), F32),
            pltpu.VMEM((D_WIN, COLS), BF16),
            dma((3,)), dma((2 * WIN,)), dma((2 + WIN // 2,)),
            dma((PEERS - 1,)), dma((PEERS - 1,)),
            dma((2,)), dma((2,)),
            dma((2, near)), dma((2, near)),
            dma((2, far)), dma((2, far)),
            dma((2, near)), dma((2, near)),
            dma((2, near + 1)), dma((2, near + 1)),
            dma((s_near,)), dma((s_near,)),
            dma((s_far,)), dma((s_far,)),
            dma((s_near,)), dma((s_near,)),
        ],
        compiler_params=pltpu.CompilerParams(
            collective_id=0, has_side_effects=True, vmem_limit_bytes=48 * 1024 * 1024
        ),
        name="powersgd",
    )(activations, out_grads, query_weight, carried_q.T)
    return summed, q_summed.T, error[None]


def solution(mesh):
    in_specs = (P("replica", None), P("replica", "tensor"), P(None, "tensor"), P("tensor", None))
    out_specs = (P(("replica", "tensor"), None), P("tensor", None), P("replica", None, "tensor"))
    return jax.shard_map(shards, mesh=mesh, in_specs=in_specs, out_specs=out_specs, check_vma=False)
```

time: 107 us -> 94.5 us (0.88)
  Pallas kernels: 99.3 us -> 86.7 us
    pallas_call x1, Pallas kernels: 99.3 us -> 86.7 us  [shards(): pl.pallas_call(kernel, out_shape=(jax.ShapeDtypeStruct((ROWS, D_WIN), BF1...]
where the time goes in v2:
time: 94.5 us; the launch traced here: 93.3 us
  Pallas kernels  86.7 us (92%)
  local copies, waits for them, and re-layouts  5.93 us (6%)
    pallas_call x1, Pallas kernels, shards(): pl.pallas_call(kernel, out_shape=(jax.ShapeDtypeStruct((ROWS, D_WIN), BF1...  86.7 us
    unnamed x9, local copies, waits for them, and re-layouts  5.93 us

profile of v2, /device:TPU:25, one launch (start us, length us, event | category | flops | bytes accessed | tf_op | source)
XLA Modules:
  0.0 93.3 jit_solution(3499515728344362479)
XLA Ops:
  0.6 0.0 copy-start
  0.6 1.6 %copy-done = bf16[256,4096]{1,0:T(8,128)(2,1)S(1)} copy-done((bf16[256,4096]{1,0:T(8,128)(2,1)S(1)}, bf16[256,4096]{1,0:T(8,128)(2,1)}, u32[]{:S(2)}) %copy-start) | copy-done | bytes 2097176
  2.2 0.0 copy-start.1
  2.2 0.9 copy-done.1
  3.1 0.0 copy-start.2
  3.1 0.8 copy-done.2
  4.0 86.7 %powersgd.1 = (bf16[16,4096]{1,0:T(8,128)(2,1)S(1)}, f32[64,256]{1,0:T(8,128)S(1)}, bf16[4096,256]{1,0:T(8,128)(2,1)S(1)}) custom-call(bf16[256,4096]{1,0:T(8,128)(2,1)S(1)} %copy-done, bf16[256,256]{1,0:T(8,128)(2,1)S(1)} %copy-done.1, bf16[4096,256]{1,0:T(8,128)(2,1)} %weight_hbm.1, f32[64,256]{1,0:T(8,128)S(1)} %bitcast.4), custom_call_target="tpu_custom_call" | custom-call | tf_op jit(solution)/shard_map/powersgd/pallas_call | solution.py:357
  90.6 0.7 copy.10
  91.3 0.6 copy.11
  91.9 1.3 %copy.12 = bf16[1,4096,256]{2,1,0:T(8,128)(2,1)} copy(bf16[1,4096,256]{2,1,0:T(8,128)(2,1)S(1)} %bitcast.3) | data formatting | bytes 4194304
Async XLA Ops:
  0.6 1.6 %copy-start = (bf16[256,4096]{1,0:T(8,128)(2,1)S(1)}, bf16[256,4096]{1,0:T(8,128)(2,1)}, u32[]{:S(2)}) copy-start(bf16[256,4096]{1,0:T(8,128)(2,1)} %act_hbm.1) | copy-start | bytes 6291460
  2.2 0.9 copy-start.1
  3.1 0.8 copy-start.2

commit v3 on v2

--- a/solution.py
+++ b/solution.py
@@ -20,7 +20,8 @@
 BLK = D_WIN // (2 * WIN)
 ROWS = TOK // PEERS
 
-HALF = RANK // 2
+PIECES = 2
+HALF = RANK // PIECES
 S_WIN = 4
 S_ROWS = RANK // (2 * S_WIN)
 
@@ -41,13 +42,13 @@
 
 def kernel(
     act_hbm, grad_hbm, weight_hbm, q_hbm,
-    summed_hbm, q_out_hbm, error_hbm,
+    summed_out, q_sum_out, right_out, gradient_out, p_cols_out,
     act, og, weight, carried, gradient, part, from_peers, summed,
     p_send, p_acc, p_pair, near_send, near_recv, mid, p_full, p_cols, z, gram, aug, apply_ref,
-    s_all, s_near_recv, s_mid, s_full, right_parts, q_out, error,
+    s_all, s_near_recv, s_mid, s_full, right_parts, q_out,
     load_sems, act_sems, store_sems, peer_send, peer_recv,
     pair_s, pair_r, near_s, near_r, mid_s, mid_r, gather_s, gather_r, pass_s, pass_r,
-    s_near_s, s_near_r, s_mid_s, s_mid_r, s_gather_s, s_gather_r,
+    s_near_s, s_near_r, s_mid_s, s_mid_r, s_gather_s, s_gather_r, far_ready,
 ):
     replica = lax.axis_index("replica")
     tensor = lax.axis_index("tensor")
@@ -90,7 +91,7 @@
         load_act(i).start()
 
     barrier = pltpu.get_barrier_semaphore()
-    friends = [at(o) for o in (16, 12, -12, 8, -8, 4, -4, 3, -3, 2, -2, 1, -1)]
+    friends = [at(o) for o in (8, -8, 4, -4, 3, -3, 2, -2, 1, -1)]
     friends += [at(o, other) for o in (2, -2, 1, -1)] + [partner]
     friends += [peer(o) for o in range(1, PEERS)]
     for friend in friends:
@@ -111,23 +112,25 @@
         for j in range(first, first + WIN // 2):
             both = dot(y_parts, act[2 * j + half], ((1,), (0,)))
             block = (both[:RANK] + both[RANK:]).astype(out.dtype)
-            out[0, j] = block[:HALF]
-            out[1, j] = block[HALF:]
+            for h in range(PIECES):
+                out[h, j] = block[h * HALF : (h + 1) * HALF]
 
     for start, half, out in ((0, other, p_send), (WIN, core, p_acc)):
         for first in (0, WIN // 2):
             p_blocks(first, start, half, out)
 
     pl.semaphore_wait(barrier, len(friends))
+    for o in (8, -8):
+        pl.semaphore_signal(far_ready, inc=1, device_id=at(o), device_id_type=MESH)
 
     pairs = []
-    for h in range(2):
+    for h in range(PIECES):
         copy = remote(p_send.at[h], p_pair.at[h], pair_s.at[h], pair_r.at[h], partner)
         copy.start()
         pairs.append(copy)
 
     sends = []
-    for h in range(2):
+    for h in range(PIECES):
         pairs[h].wait_recv()
         for k, e in enumerate(NEAR):
             j = lax.rem(chip_at(sign * e), WIN)
@@ -155,7 +158,9 @@
 
     order = list(reversed(range(len(NEAR))))
     mid_copies = []
-    for h in range(2):
+    for h in range(PIECES):
+        if h == 0:
+            pl.semaphore_wait(far_ready, 2)
         total = p_acc[h, mine] + p_pair[h, mine].astype(F32)
         for k in order:
             sends[h * len(NEAR) + k].wait_recv()
@@ -170,6 +175,9 @@
     def _(b):
         gradient[b] = dot(act[b], og[...], ((0,), (0,)))
 
+    store_gradient = pltpu.make_async_copy(gradient, gradient_out, store_sems.at[2])
+    store_gradient.start()
+
     def gather_from(k):
         return lax.rem(chip_at(sign * NEAR[k]), WIN)
 
@@ -180,7 +188,7 @@
         copy.start()
         passes.append(copy)
 
-    for h in range(2):
+    for h in range(PIECES):
         for k in range(len(FAR)):
             mid_copies[h * len(FAR) + k].wait_recv()
         chunk = mid[h, 0].astype(F32)
@@ -206,7 +214,7 @@
 
     z[...] = jnp.zeros_like(z)
     gram[...] = jnp.zeros_like(gram)
-    for h in range(2):
+    for h in range(PIECES):
         for k in order:
             j = gather_from(k)
             remote(
@@ -219,7 +227,7 @@
         z_gram(core, j)
     for k in [len(NEAR)] + order:
         j = mine if k == len(NEAR) else lax.rem(chip_at(-sign * NEAR[k]), WIN)
-        for h in range(2):
+        for h in range(PIECES):
             remote(
                 p_full.at[other, j, h], p_full.at[other, j, h], pass_s.at[h, k], pass_r.at[h, k], partner
             ).wait_recv()
@@ -256,6 +264,9 @@
     def _(b):
         block = p_whole(lax.rem(b, 2), b // 2)
         p_cols[b] = jnp.concatenate([block, block], axis=0).T
+
+    store_p_cols = pltpu.make_async_copy(p_cols, p_cols_out, store_sems.at[3])
+    store_p_cols.start()
 
     s_total = s_all[s_rows(s_mine)]
     for k in reversed(range(len(s_targets))):
@@ -312,7 +323,7 @@
             acc += from_peers[t, :, columns].astype(F32)
         summed[:, columns] = acc.astype(BF16)
 
-    store_summed = pltpu.make_async_copy(summed, summed_hbm, store_sems.at[0])
+    store_summed = pltpu.make_async_copy(summed, summed_out, store_sems.at[0])
     store_summed.start()
 
     for k in reversed(range(len(s_targets))):
@@ -326,43 +337,55 @@
     both = dot(apply_ref[...], s_full[...].reshape(RANK, COLS), ((1,), (0,)), highest)
     right_high, right_low = halves(both[RANK:])
     right_parts[...] = jnp.concatenate([right_high, right_low], axis=0)
-
+    store_right = pltpu.make_async_copy(right_parts, right_out, store_sems.at[4])
+    store_right.start()
     q_out[...] = both[:RANK]
-    store_q = pltpu.make_async_copy(q_out, q_out_hbm, store_sems.at[1])
+    store_q = pltpu.make_async_copy(q_out, q_sum_out, store_sems.at[1])
     store_q.start()
 
-    def store_error(g):
-        rows = pl.ds(g * 4 * BLK, 4 * BLK)
-        return pltpu.make_async_copy(error.at[rows], error_hbm.at[rows], store_sems.at[2 + g])
-
+    for copy in pairs + sends + mid_copies + gathers + passes + peer_copies + s_sends + s_mid_copies + s_gathers:
+        copy.wait_send()
+    for copy in (store_summed, store_gradient, store_p_cols, store_right, store_q):
+        copy.wait()
+
+
+def finish(
+    summed, q_summed, right_parts, gradient, p_cols, summed_hbm, q_hbm, error_hbm, error, sems
+):
+    store_summed = pltpu.make_async_copy(summed, summed_hbm, sems.at[0])
+    store_q = pltpu.make_async_copy(q_summed, q_hbm, sems.at[1])
+    store_summed.start()
+    store_q.start()
+    stores = []
     for g in range(WIN // 2):
         for b in range(4 * g, 4 * g + 4):
             product = dot(p_cols[b], right_parts[...], ((1,), (0,)))
             error[pl.ds(b * BLK, BLK), :] = (gradient[b] - product).astype(BF16)
-        store_error(g).start()
-
-    for copy in pairs + sends + mid_copies + gathers + passes + peer_copies + s_sends + s_mid_copies + s_gathers:
-        copy.wait_send()
-    store_summed.wait()
-    store_q.wait()
-
-    for g in range(WIN // 2):
-        store_error(g).wait()
+        rows = pl.ds(g * 4 * BLK, 4 * BLK)
+        stores.append(pltpu.make_async_copy(error.at[rows], error_hbm.at[rows], sems.at[2 + g]))
+        stores[-1].start()
+    for copy in [store_summed, store_q] + stores:
+        copy.wait()
 
 
 def shards(activations, out_grads, query_weight, carried_q):
     in_hbm = pl.BlockSpec(memory_space=pltpu.HBM)
     dma = pltpu.SemaphoreType.DMA
     near, far, s_near, s_far = len(NEAR), len(FAR), 2 * len(S_NEAR) + 1, len(S_FAR)
-    summed, q_summed, error = pl.pallas_call(
+    passed = (
+        jax.ShapeDtypeStruct((ROWS, D_WIN), BF16),
+        jax.ShapeDtypeStruct((RANK, COLS), F32),
+        jax.ShapeDtypeStruct((2 * RANK, COLS), BF16),
+        jax.ShapeDtypeStruct((2 * WIN, BLK, COLS), F32),
+        jax.ShapeDtypeStruct((2 * WIN, BLK, 2 * RANK), BF16),
+    )
+    operands = (activations, out_grads, query_weight, carried_q.T)
+    inputs = [pltpu.with_memory_space_constraint(x, pltpu.HBM) for x in operands]
+    results = pl.pallas_call(
         kernel,
-        out_shape=(
-            jax.ShapeDtypeStruct((ROWS, D_WIN), BF16),
-            jax.ShapeDtypeStruct((RANK, COLS), F32),
-            jax.ShapeDtypeStruct((D_WIN, COLS), BF16),
-        ),
+        out_shape=passed,
         in_specs=[in_hbm] * 4,
-        out_specs=(pl.BlockSpec(memory_space=pl.ANY),) * 3,
+        out_specs=(pl.BlockSpec(memory_space=pl.ANY),) * len(passed),
         scratch_shapes=[
             pltpu.VMEM((2 * WIN, TOK, BLK), BF16),
             pltpu.VMEM((TOK, COLS), BF16),
@@ -372,13 +395,13 @@
             pltpu.VMEM((TOK, D_WIN), BF16),
             pltpu.VMEM((PEERS, ROWS, D_WIN), BF16),
             pltpu.VMEM((ROWS, D_WIN), BF16),
-            pltpu.VMEM((2, WIN, HALF, BLK), BF16),
-            pltpu.VMEM((2, WIN, HALF, BLK), F32),
-            pltpu.VMEM((2, WIN, HALF, BLK), BF16),
-            pltpu.VMEM((2, near, HALF, BLK), BF16),
-            pltpu.VMEM((2, near, HALF, BLK), BF16),
-            pltpu.VMEM((2, GROUPS, HALF, BLK), BF16),
-            pltpu.VMEM((2, WIN, 2, HALF, BLK), BF16),
+            pltpu.VMEM((PIECES, WIN, HALF, BLK), BF16),
+            pltpu.VMEM((PIECES, WIN, HALF, BLK), F32),
+            pltpu.VMEM((PIECES, WIN, HALF, BLK), BF16),
+            pltpu.VMEM((PIECES, near, HALF, BLK), BF16),
+            pltpu.VMEM((PIECES, near, HALF, BLK), BF16),
+            pltpu.VMEM((PIECES, GROUPS, HALF, BLK), BF16),
+            pltpu.VMEM((2, WIN, PIECES, HALF, BLK), BF16),
             pltpu.VMEM((2 * WIN, BLK, 2 * RANK), BF16),
             pltpu.VMEM((RANK, TOK), F32),
             pltpu.VMEM((RANK, RANK), F32),
@@ -390,23 +413,32 @@
             pltpu.VMEM((2 * S_WIN, S_ROWS, COLS), F32),
             pltpu.VMEM((2 * RANK, COLS), BF16),
             pltpu.VMEM((RANK, COLS), F32),
-            pltpu.VMEM((D_WIN, COLS), BF16),
-            dma((3,)), dma((2 * WIN,)), dma((2 + WIN // 2,)),
+            dma((3,)), dma((2 * WIN,)), dma((5,)),
             dma((PEERS - 1,)), dma((PEERS - 1,)),
-            dma((2,)), dma((2,)),
-            dma((2, near)), dma((2, near)),
-            dma((2, far)), dma((2, far)),
-            dma((2, near)), dma((2, near)),
-            dma((2, near + 1)), dma((2, near + 1)),
+            dma((PIECES,)), dma((PIECES,)),
+            dma((PIECES, near)), dma((PIECES, near)),
+            dma((PIECES, far)), dma((PIECES, far)),
+            dma((PIECES, near)), dma((PIECES, near)),
+            dma((PIECES, near + 1)), dma((PIECES, near + 1)),
             dma((s_near,)), dma((s_near,)),
             dma((s_far,)), dma((s_far,)),
             dma((s_near,)), dma((s_near,)),
+            pltpu.SemaphoreType.REGULAR,
         ],
         compiler_params=pltpu.CompilerParams(
-            collective_id=0, has_side_effects=True, vmem_limit_bytes=48 * 1024 * 1024
+            collective_id=0, has_side_effects=True, vmem_limit_bytes=28 * 1024 * 1024
         ),
         name="powersgd",
-    )(activations, out_grads, query_weight, carried_q.T)
+    )(*inputs)
+    summed, q_summed, error = pl.pallas_call(
+        finish,
+        out_shape=(passed[0], passed[1], jax.ShapeDtypeStruct((D_WIN, COLS), BF16)),
+        in_specs=[pl.BlockSpec(memory_space=pltpu.VMEM)] * len(passed),
+        out_specs=(pl.BlockSpec(memory_space=pl.ANY),) * 3,
+        scratch_shapes=[pltpu.VMEM((D_WIN, COLS), BF16), dma((2 + WIN // 2,))],
+        compiler_params=pltpu.CompilerParams(vmem_limit_bytes=24 * 1024 * 1024),
+        name="finish",
+    )(*results)
     return summed, q_summed.T, error[None]
 
 

time: 94.5 us -> 82.4 us (0.87)
  the two profiles are of different devices: /device:TPU:25 before, /device:TPU:3 now
where the time goes in v3:
time: 82.4 us; the launch traced here: 82.2 us
  Pallas kernels  81.6 us (99%)
    pallas_call x1, Pallas kernels, shards(): pl.pallas_call(kernel, out_shape=passed, in_specs=[in_hbm] * 4, out_specs...  79.9 us
    pallas_call x1, Pallas kernels, shards(): pl.pallas_call(finish, out_shape=(passed[0], passed[1], jax.ShapeDtypeStr...  1.65 us

profile of v3, /device:TPU:3, one launch (start us, length us, event | category | flops | bytes accessed | tf_op | source)
XLA Modules:
  0.0 82.2 jit_solution(1486755907417770468)
XLA Ops:
  0.6 79.9 %powersgd.1 = (bf16[16,4096]{1,0:T(8,128)(2,1)S(1)}, f32[64,256]{1,0:T(8,128)S(1)}, bf16[128,256]{1,0:T(8,128)(2,1)S(1)}, f32[16,256,256]{2,1,0:T(8,128)S(1)}, bf16[16,256,128]{2,1,0:T(8,128)(2,1)S(1)}) custom-call(bf16[256,4096]{1,0:T(8,128)(2,1)} %act_hbm.1, bf16[256,256]{1,0:T(8,128)(2,1)} %grad_hbm.1, bf16[4096,256]{1,0:T(8,128)(2,1)} %weight_hbm.1, ...), custom_call_target="tpu_custom_call" | custom-call | tf_op jit(solution)/shard_map/powersgd/pallas_call | solution.py:384
  80.6 1.7 %finish.1 = (bf16[16,4096]{1,0:T(8,128)(2,1)}, f32[64,256]{1,0:T(8,128)}, bf16[4096,256]{1,0:T(8,128)(2,1)}) custom-call(bf16[16,4096]{1,0:T(8,128)(2,1)S(1)} %get-tuple-element.11.summed, f32[64,256]{1,0:T(8,128)S(1)} %get-tuple-element.12.q_summed, bf16[128,256]{1,0:T(8,128)(2,1)S(1)} %get-tuple-element.13.right_parts, ...), custom_call_target="tpu_custom_call" | custom-call | tf_op jit(solution)/shard_map/finish/pallas_call | solution.py:433

commit v4 on v3

--- a/solution.py
+++ b/solution.py
@@ -43,11 +43,11 @@
 def kernel(
     act_hbm, grad_hbm, weight_hbm, q_hbm,
     summed_out, q_sum_out, right_out, gradient_out, p_cols_out,
-    act, og, weight, carried, gradient, part, from_peers, summed,
+    act, act_pair, og_pair, og, weight, carried, gradient, part, from_peers, summed,
     p_send, p_acc, p_pair, near_send, near_recv, mid, p_full, p_cols, z, gram, aug, apply_ref,
     s_all, s_near_recv, s_mid, s_full, right_parts, q_out,
     load_sems, act_sems, store_sems, peer_send, peer_recv,
-    pair_s, pair_r, near_s, near_r, mid_s, mid_r, gather_s, gather_r, pass_s, pass_r,
+    swap_s, swap_r, pair_s, pair_r, near_s, near_r, mid_s, mid_r, gather_s, gather_r, pass_s, pass_r,
     s_near_s, s_near_r, s_mid_s, s_mid_r, s_gather_s, s_gather_r, far_ready,
 ):
     replica = lax.axis_index("replica")
@@ -84,7 +84,7 @@
     def load_act(index):
         half, j = index // WIN, lax.rem(index, WIN)
         b = 2 * j + lax.rem(half + other, 2)
-        return pltpu.make_async_copy(act_hbm.at[:, pl.ds(b * BLK, BLK)], act.at[b], act_sems.at[index])
+        return pltpu.make_async_copy(act_hbm.at[:, pl.ds(b * BLK, BLK)], act.at[lax.rem(half + other, 2), j], act_sems.at[index])
 
     @pl.loop(0, 2 * WIN)
     def _(i):
@@ -110,7 +110,7 @@
         for j in range(first, first + WIN // 2):
             load_act(start + j).wait()
         for j in range(first, first + WIN // 2):
-            both = dot(y_parts, act[2 * j + half], ((1,), (0,)))
+            both = dot(y_parts, act[half, j], ((1,), (0,)))
             block = (both[:RANK] + both[RANK:]).astype(out.dtype)
             for h in range(PIECES):
                 out[h, j] = block[h * HALF : (h + 1) * HALF]
@@ -139,22 +139,12 @@
             copy.start()
             sends.append(copy)
 
-    load_weight.wait()
-
-    @pl.loop(0, D_WIN // COLS, unroll=4)
-    def _(b):
-        rows = pl.ds(pl.multiple_of(b * COLS, COLS), COLS)
-        part[:, rows] = dot(og[...], weight[rows, :], ((1,), (1,))).astype(BF16)
-
-    peer_copies = []
-    for o in range(1, PEERS):
-        to = lax.rem(tensor + o, PEERS)
-        copy = remote(
-            part.at[pl.ds(pl.multiple_of(to * ROWS, ROWS), ROWS)], from_peers.at[tensor],
-            peer_send.at[o - 1], peer_recv.at[o - 1], peer(o),
-        )
-        copy.start()
-        peer_copies.append(copy)
+    swaps = [
+        remote(act.at[other], act_pair, swap_s.at[0], swap_r.at[0], partner),
+        remote(og, og_pair, swap_s.at[1], swap_r.at[1], partner),
+    ]
+    for copy in swaps:
+        copy.start()
 
     order = list(reversed(range(len(NEAR))))
     mid_copies = []
@@ -171,9 +161,26 @@
             copy.start()
             mid_copies.append(copy)
 
+    load_weight.wait()
+
+    @pl.loop(0, D_WIN // COLS, unroll=4)
+    def _(b):
+        rows = pl.ds(pl.multiple_of(b * COLS, COLS), COLS)
+        part[:, rows] = dot(og[...], weight[rows, :], ((1,), (1,))).astype(BF16)
+
+    peer_copies = []
+    for o in range(1, PEERS):
+        to = lax.rem(tensor + o, PEERS)
+        copy = remote(
+            part.at[pl.ds(pl.multiple_of(to * ROWS, ROWS), ROWS)], from_peers.at[tensor],
+            peer_send.at[o - 1], peer_recv.at[o - 1], peer(o),
+        )
+        copy.start()
+        peer_copies.append(copy)
+
     @pl.loop(0, D_WIN // BLK, unroll=4)
     def _(b):
-        gradient[b] = dot(act[b], og[...], ((0,), (0,)))
+        gradient[b] = dot(act[lax.rem(b, 2), b // 2], og[...], ((0,), (0,)))
 
     store_gradient = pltpu.make_async_copy(gradient, gradient_out, store_sems.at[2])
     store_gradient.start()
@@ -207,13 +214,14 @@
     def p_whole(half, j):
         return p_full[half, j].reshape(RANK, BLK)
 
-    def z_gram(half, j):
+    def add_gram(half, j):
         block = p_whole(half, j)
-        z[...] += dot(block, act[2 * j + half], ((1,), (1,)))
         gram[...] += dot(block, block, ((1,), (1,)))
 
     z[...] = jnp.zeros_like(z)
     gram[...] = jnp.zeros_like(gram)
+    for copy in swaps:
+        copy.wait_recv()
     for h in range(PIECES):
         for k in order:
             j = gather_from(k)
@@ -222,19 +230,14 @@
                 at(sign * NEAR[k]),
             ).wait_recv()
             hand_on(h, k, j)
-    for k in [len(NEAR)] + order:
-        j = mine if k == len(NEAR) else gather_from(k)
-        z_gram(core, j)
-    for k in [len(NEAR)] + order:
-        j = mine if k == len(NEAR) else lax.rem(chip_at(-sign * NEAR[k]), WIN)
-        for h in range(PIECES):
-            remote(
-                p_full.at[other, j, h], p_full.at[other, j, h], pass_s.at[h, k], pass_r.at[h, k], partner
-            ).wait_recv()
-        z_gram(other, j)
+    for j in range(WIN):
+        block = p_whole(core, j)
+        z[:, :TOK] += dot(block, act[core, j], ((1,), (1,)))
+        z[:, TOK:] += dot(block, act_pair[j], ((1,), (1,)))
 
     z_high, z_low = halves(z[...])
-    s2 = dot(jnp.concatenate([z_high, z_low], axis=0), og[...], ((1,), (0,)))
+    z_parts = jnp.concatenate([z_high, z_low], axis=0)
+    s2 = dot(z_parts[:, :TOK], og[...], ((1,), (0,))) + dot(z_parts[:, TOK:], og_pair[...], ((1,), (0,)))
     s_all[...] = s2[:RANK] + s2[RANK:]
 
     s_targets = [(e, core) for e in S_NEAR] + [(e, other) for e in S_NEAR] + [(0, other)]
@@ -256,6 +259,16 @@
         copy.start()
         s_sends.append(copy)
 
+    for k in [len(NEAR)] + order:
+        j = mine if k == len(NEAR) else lax.rem(chip_at(-sign * NEAR[k]), WIN)
+        for h in range(PIECES):
+            remote(
+                p_full.at[other, j, h], p_full.at[other, j, h], pass_s.at[h, k], pass_r.at[h, k], partner
+            ).wait_recv()
+
+    for half in range(2):
+        for j in range(WIN):
+            add_gram(half, j)
     lane = lax.broadcasted_iota(jnp.int32, (RANK, 2 * RANK), 1)
     row = lax.broadcasted_iota(jnp.int32, (RANK, 2 * RANK), 0)
     aug[...] = jnp.concatenate([gram[...], (lane == row)[:, :RANK].astype(F32)], axis=1)
@@ -343,7 +356,7 @@
     store_q = pltpu.make_async_copy(q_out, q_sum_out, store_sems.at[1])
     store_q.start()
 
-    for copy in pairs + sends + mid_copies + gathers + passes + peer_copies + s_sends + s_mid_copies + s_gathers:
+    for copy in swaps + pairs + sends + mid_copies + gathers + passes + peer_copies + s_sends + s_mid_copies + s_gathers:
         copy.wait_send()
     for copy in (store_summed, store_gradient, store_p_cols, store_right, store_q):
         copy.wait()
@@ -357,11 +370,11 @@
     store_summed.start()
     store_q.start()
     stores = []
-    for g in range(WIN // 2):
-        for b in range(4 * g, 4 * g + 4):
+    for g in range(WIN):
+        for b in range(2 * g, 2 * g + 2):
             product = dot(p_cols[b], right_parts[...], ((1,), (0,)))
             error[pl.ds(b * BLK, BLK), :] = (gradient[b] - product).astype(BF16)
-        rows = pl.ds(g * 4 * BLK, 4 * BLK)
+        rows = pl.ds(g * 2 * BLK, 2 * BLK)
         stores.append(pltpu.make_async_copy(error.at[rows], error_hbm.at[rows], sems.at[2 + g]))
         stores[-1].start()
     for copy in [store_summed, store_q] + stores:
@@ -387,7 +400,9 @@
         in_specs=[in_hbm] * 4,
         out_specs=(pl.BlockSpec(memory_space=pl.ANY),) * len(passed),
         scratch_shapes=[
-            pltpu.VMEM((2 * WIN, TOK, BLK), BF16),
+            pltpu.VMEM((2, WIN, TOK, BLK), BF16),
+            pltpu.VMEM((WIN, TOK, BLK), BF16),
+            pltpu.VMEM((TOK, COLS), BF16),
             pltpu.VMEM((TOK, COLS), BF16),
             pltpu.VMEM((D_WIN, COLS), BF16),
             pltpu.VMEM((RANK, COLS), F32),
@@ -403,7 +418,7 @@
             pltpu.VMEM((PIECES, GROUPS, HALF, BLK), BF16),
             pltpu.VMEM((2, WIN, PIECES, HALF, BLK), BF16),
             pltpu.VMEM((2 * WIN, BLK, 2 * RANK), BF16),
-            pltpu.VMEM((RANK, TOK), F32),
+            pltpu.VMEM((RANK, 2 * TOK), F32),
             pltpu.VMEM((RANK, RANK), F32),
             pltpu.VMEM((RANK, 2 * RANK), F32),
             pltpu.VMEM((2 * RANK, RANK), F32),
@@ -415,6 +430,7 @@
             pltpu.VMEM((RANK, COLS), F32),
             dma((3,)), dma((2 * WIN,)), dma((5,)),
             dma((PEERS - 1,)), dma((PEERS - 1,)),
+            dma((2,)), dma((2,)),
             dma((PIECES,)), dma((PIECES,)),
             dma((PIECES, near)), dma((PIECES, near)),
             dma((PIECES, far)), dma((PIECES, far)),
@@ -435,7 +451,7 @@
         out_shape=(passed[0], passed[1], jax.ShapeDtypeStruct((D_WIN, COLS), BF16)),
         in_specs=[pl.BlockSpec(memory_space=pltpu.VMEM)] * len(passed),
         out_specs=(pl.BlockSpec(memory_space=pl.ANY),) * 3,
-        scratch_shapes=[pltpu.VMEM((D_WIN, COLS), BF16), dma((2 + WIN // 2,))],
+        scratch_shapes=[pltpu.VMEM((D_WIN, COLS), BF16), dma((2 + WIN,))],
         compiler_params=pltpu.CompilerParams(vmem_limit_bytes=24 * 1024 * 1024),
         name="finish",
     )(*results)

time: 82.4 us -> 81 us (0.983)
  the two profiles are of different devices: /device:TPU:3 before, /device:TPU:25 now
where the time goes in v4:
time: 81 us; the launch traced here: 80.8 us
  Pallas kernels  80.2 us (99%)
    pallas_call x1, Pallas kernels, shards(): pl.pallas_call(kernel, out_shape=passed, in_specs=[in_hbm] * 4, out_specs...  78.6 us

profile of v4, /device:TPU:25, one launch (start us, length us, event | category | flops | bytes accessed | tf_op | source)
XLA Modules:
  0.0 80.8 jit_solution(16491454651459889415)
XLA Ops:
  0.6 78.6 %powersgd.1 = (bf16[16,4096]{1,0:T(8,128)(2,1)S(1)}, f32[64,256]{1,0:T(8,128)S(1)}, bf16[128,256]{1,0:T(8,128)(2,1)S(1)}, f32[16,256,256]{2,1,0:T(8,128)S(1)}, bf16[16,256,128]{2,1,0:T(8,128)(2,1)S(1)}) custom-call(bf16[256,4096]{1,0:T(8,128)(2,1)} %act_hbm.1, bf16[256,256]{1,0:T(8,128)(2,1)} %grad_hbm.1, bf16[4096,256]{1,0:T(8,128)(2,1)} %weight_hbm.1, ...), custom_call_target="tpu_custom_call" | custom-call | tf_op jit(solution)/shard_map/powersgd/pallas_call | solution.py:397
  79.2 1.6 %finish.1 = (bf16[16,4096]{1,0:T(8,128)(2,1)}, f32[64,256]{1,0:T(8,128)}, bf16[4096,256]{1,0:T(8,128)(2,1)}) custom-call(bf16[16,4096]{1,0:T(8,128)(2,1)S(1)} %get-tuple-element.11.summed, f32[64,256]{1,0:T(8,128)S(1)} %get-tuple-element.12.q_summed, bf16[128,256]{1,0:T(8,128)(2,1)S(1)} %get-tuple-element.13.right_parts, ...), custom_call_target="tpu_custom_call" | custom-call | tf_op jit(solution)/shard_map/finish/pallas_call | solution.py:449

commit v5 on v4

--- a/solution.py
+++ b/solution.py
@@ -311,6 +311,21 @@
     )
 
     apply_ref[...] = apply
+    from_peers[tensor] = part[pl.ds(pl.multiple_of(tensor * ROWS, ROWS), ROWS), :]
+    for copy in peer_copies:
+        copy.wait_recv()
+
+    @pl.loop(0, D_WIN // 512, unroll=2)
+    def _(i):
+        columns = pl.ds(pl.multiple_of(i * 512, 512), 512)
+        acc = from_peers[0, :, columns].astype(F32)
+        for t in range(1, PEERS):
+            acc += from_peers[t, :, columns].astype(F32)
+        summed[:, columns] = acc.astype(BF16)
+
+    store_summed = pltpu.make_async_copy(summed, summed_out, store_sems.at[0])
+    store_summed.start()
+
     for copy in s_mid_copies:
         copy.wait_recv()
     s_chunk = s_mid[0]
@@ -324,21 +339,6 @@
         )
         copy.start()
         s_gathers.append(copy)
-    from_peers[tensor] = part[pl.ds(pl.multiple_of(tensor * ROWS, ROWS), ROWS), :]
-    for copy in peer_copies:
-        copy.wait_recv()
-
-    @pl.loop(0, D_WIN // 512, unroll=2)
-    def _(i):
-        columns = pl.ds(pl.multiple_of(i * 512, 512), 512)
-        acc = from_peers[0, :, columns].astype(F32)
-        for t in range(1, PEERS):
-            acc += from_peers[t, :, columns].astype(F32)
-        summed[:, columns] = acc.astype(BF16)
-
-    store_summed = pltpu.make_async_copy(summed, summed_out, store_sems.at[0])
-    store_summed.start()
-
     for k in reversed(range(len(s_targets))):
         e, on = s_targets[k]
         toward = sign * e if k < len(S_NEAR) else -sign * e

time: 81 us -> 83.1 us (1.026); the launches traced: 80.8 us -> 81.6 us
  no operation moved by 1% of the time
where the time goes in v5:
time: 83.1 us; the launch traced here: 81.6 us
  Pallas kernels  81 us (97%)
    pallas_call x1, Pallas kernels, shards(): pl.pallas_call(kernel, out_shape=passed, in_specs=[in_hbm] * 4, out_specs...  79.4 us

profile of v5, /device:TPU:25, one launch (start us, length us, event | category | flops | bytes accessed | tf_op | source)
XLA Modules:
  0.0 81.6 jit_solution(6775099778160868548)
XLA Ops:
  0.6 79.4 %powersgd.1 = (bf16[16,4096]{1,0:T(8,128)(2,1)S(1)}, f32[64,256]{1,0:T(8,128)S(1)}, bf16[128,256]{1,0:T(8,128)(2,1)S(1)}, f32[16,256,256]{2,1,0:T(8,128)S(1)}, bf16[16,256,128]{2,1,0:T(8,128)(2,1)S(1)}) custom-call(bf16[256,4096]{1,0:T(8,128)(2,1)} %act_hbm.1, bf16[256,256]{1,0:T(8,128)(2,1)} %grad_hbm.1, bf16[4096,256]{1,0:T(8,128)(2,1)} %weight_hbm.1, ...), custom_call_target="tpu_custom_call" | custom-call | tf_op jit(solution)/shard_map/powersgd/pallas_call | solution.py:397
  80.0 1.6 %finish.1 = (bf16[16,4096]{1,0:T(8,128)(2,1)}, f32[64,256]{1,0:T(8,128)}, bf16[4096,256]{1,0:T(8,128)(2,1)}) custom-call(bf16[16,4096]{1,0:T(8,128)(2,1)S(1)} %get-tuple-element.11.summed, f32[64,256]{1,0:T(8,128)S(1)} %get-tuple-element.12.q_summed, bf16[128,256]{1,0:T(8,128)(2,1)S(1)} %get-tuple-element.13.right_parts, ...), custom_call_target="tpu_custom_call" | custom-call | tf_op jit(solution)/shard_map/finish/pallas_call | solution.py:449
